TPU v7x, 32 devices: a whole 2x2x4 slice. The times are simulated.
32 devices in a mesh: run: 2 (over core), ctx: 4 (over z), head: 4 (over y, x).
Axes of the slice: x: 2, y: 2, z: 4, core: 2. Of those that a mesh axis runs over, the one named last changes fastest.
Arguments:
- inner_tokens: bfloat16 [16384, 5120], P(('run', 'ctx', 'head')), parts along dimension 0, may hold values from -6 to 6
- state_inputs: bfloat16 [16384, 256], P(('run', 'ctx', 'head')), parts along dimension 0, may hold values from -6 to 6
- step_raw: bfloat16 [16384, 80], P(('run', 'ctx', 'head')), parts along dimension 0, may hold values from -3 to 24
- conv_inner: float32 [5, 5120], P(None, 'head'), may hold values from -3 to 3
- conv_state: float32 [5, 256], replicated, may hold values from -3 to 3
- head_rates: float32 [4, 80], P('run', 'head'), parts along dimension 0, may hold values from -15 to 4
- skip_gain: float32 [80], P('head'), may hold values from 0.5 to 1.5
Outputs:
- mixed: bfloat16 [16384, 5120], P(('run', 'ctx', 'head')), parts along dimension 0
There are 2 independent parts, one for each index of `run`. A program takes and returns all parts, laid end to end along the dimension named above; an argument that names none is the same for every part. Nothing has to cross between parts.
All inputs are finite; a program needn't handle non-finite values.
Results may differ from a plain program's by a relative error of at most 0.009.
Values may be sent and summed in bfloat16 or wider, within the bound.
A program may use at most 192 MiB of HBM per device.

v0:
```python
import jax
import jax.numpy as jnp
from jax import lax
from jax.sharding import PartitionSpec as P

KERNEL = 4
SPAN = 256


def from_behind(value, axis, by):
    length = lax.axis_size(axis)
    pairs = [(i, i + by) for i in range(length) if 0 <= i + by < length]
    return lax.ppermute(value, axis, pairs)


def silu_conv(signal, previous_rows, kernel_taps):
    length = signal.shape[0]
    channels = signal.shape[1]
    padded = jnp.concatenate(
        [previous_rows.astype(jnp.float32), signal.astype(jnp.float32)], axis=0
    )
    summed = jnp.zeros((length, channels), jnp.float32) + kernel_taps[KERNEL][None, :]
    for offset in range(KERNEL):
        summed = summed + kernel_taps[offset][None, :] * padded[offset : offset + length]
    return jax.nn.silu(summed).astype(jnp.bfloat16)


def block_terms(carry_state, pieces):
    c_block, b_block, u_block, decay_block = pieces
    cumulative = jnp.cumsum(decay_block, axis=0)
    across = cumulative.T
    inner_scores = jnp.dot(c_block, b_block.T, preferred_element_type=jnp.float32)
    spread = across[:, :, None] - across[:, None, :]
    places = jnp.arange(c_block.shape[0])
    causal = places[:, None] >= places[None, :]
    mixing = (inner_scores[None] * jnp.exp(jnp.where(causal[None], spread, -jnp.inf))).astype(
        jnp.bfloat16
    )
    local_terms = jnp.einsum("hts,shp->thp", mixing, u_block, preferred_element_type=jnp.float32)
    carried = jnp.exp(cumulative)[:, :, None] * jnp.einsum(
        "tn,hpn->thp", c_block.astype(jnp.float32), carry_state, precision=lax.Precision.HIGHEST
    )
    ending = cumulative[-1]
    weights = jnp.exp(ending[None, :] - cumulative)
    scaled = weights[:, :, None] * u_block.astype(jnp.float32)
    new_state = jnp.exp(ending)[:, None, None] * carry_state + jnp.einsum(
        "shp,sn->hpn", scaled, b_block.astype(jnp.float32), precision=lax.Precision.HIGHEST
    )
    return (new_state, local_terms + carried)


def per_device(inner_tokens, state_inputs, step_raw, conv_inner, conv_state, head_rates, skip_gain):
    x_local, step_local = (
        lax.all_to_all(inner_tokens, "head", split_axis=1, concat_axis=0, tiled=True),
        lax.all_to_all(step_raw, "head", split_axis=1, concat_axis=0, tiled=True),
    )
    context = x_local.shape[0]
    channels = x_local.shape[1]
    heads_local = head_rates.shape[1]
    head_width = channels // heads_local
    margin_rows = KERNEL - 1
    state_whole = lax.all_gather(state_inputs, "head", axis=0, tiled=True)
    edge_rows = jnp.concatenate(
        [x_local[context - margin_rows :], state_whole[context - margin_rows :]], axis=1
    )
    previous_rows = from_behind(edge_rows, "ctx", 1)
    x_previous = previous_rows[:, :channels]
    state_conv = silu_conv(state_whole, previous_rows[:, channels:], conv_state)
    inner_conv = silu_conv(x_local, x_previous, conv_inner)
    state_width = state_conv.shape[1] // 2
    b_rows = state_conv[:, :state_width]
    c_rows = state_conv[:, state_width:]
    step_size = jax.nn.softplus(step_local.astype(jnp.float32) + head_rates[0][None, :])
    log_decay = -step_size * jnp.exp(head_rates[1])[None, :]
    x_heads = inner_conv.reshape(context, heads_local, head_width)
    inputs = (x_heads.astype(jnp.float32) * step_size[:, :, None]).astype(jnp.bfloat16)
    block_count = context // SPAN
    start_state = jnp.zeros((heads_local, head_width, state_width), jnp.float32)
    final_state, outputs = lax.scan(
        block_terms,
        start_state,
        (
            c_rows.reshape(block_count, SPAN, state_width),
            b_rows.reshape(block_count, SPAN, state_width),
            inputs.reshape(block_count, SPAN, heads_local, head_width),
            log_decay.reshape(block_count, SPAN, heads_local),
        ),
    )
    running = jnp.cumsum(log_decay, axis=0)
    device_decay = jnp.exp(running[-1])

    def relay(position, arriving):
        return from_behind(device_decay[:, None, None] * arriving + final_state, "ctx", 1)

    incoming = lax.fori_loop(0, lax.axis_size("ctx") - 1, relay, jnp.zeros_like(final_state))
    carried = jnp.exp(running)[:, :, None] * jnp.einsum(
        "tn,hpn->thp", c_rows.astype(jnp.float32), incoming, precision=lax.Precision.HIGHEST
    )
    summed = (
        outputs.reshape(context, heads_local, head_width)
        + carried
        + skip_gain[None, :, None] * x_heads.astype(jnp.float32)
    )
    regrouped = summed.astype(jnp.bfloat16).reshape(context, channels)
    return lax.all_to_all(regrouped, "head", split_axis=0, concat_axis=1, tiled=True)


def solution(mesh):
    return jax.shard_map(
        per_device,
        mesh=mesh,
        in_specs=(
            P(("run", "ctx", "head"), None),
            P(("run", "ctx", "head"), None),
            P(("run", "ctx", "head"), None),
            P(None, "head"),
            P(),
            P("run", "head"),
            P("head"),
        ),
        out_specs=P(("run", "ctx", "head"), None),
        check_vma=False,
    )
```

profile of v0, /device:TPU:28, one launch (start us, length us, event | category | flops | bytes accessed | tf_op | source)
XLA Modules:
  0.0 610.3 jit_solution(11044556583941287136)
XLA Ops:
  31.1 46.5 %all-gather.2.cloned.1.call-done = bf16[2048,256]{1,0:T(8,128)(2,1)} async-done(((bf16[512,256]{1,0:T(8,128)(2,1)}), bf16[2048,256]{1,0:T(8,128)(2,1)}) %all-gather.2.cloned.1.call-update) | async-done | bytes 1048592 | tf_op jit(solution)/shard_map/all_gather | solution.py:62
  79.7 9.5 %all-to-all-done.1 = bf16[512,4,1280]{2,0,1:T(8,128)(2,1)} async-done(((bf16[512,4,1280]{2,0,1:T(8,128)(2,1)}), bf16[512,4,1280]{2,0,1:T(8,128)(2,1)}, u32[]{:S(2)}, u32[]{:S(2)}) %all-to-all-start.1) | async-done | bytes 5242912 | tf_op jit(solution)/shard_map/all_to_all | solution.py:54
  95.5 8.2 %fusion.47 = f32[2048,1280]{1,0:T(8,128)} fusion(f32[2048,1280]{1,0:T(8,128)S(1)} %bitcast_convert_fusion, f32[1280]{0:T(1024)S(1)} %get-tuple-element.130, f32[3,1280]{1,0:T(4,128)S(1)} %slice_convert_fusion, f32[1280]{0:T(1024)S(1)} %get-tuple-element.131, f32[1280]{0:T(1024)S(1)} %get-tuple-element.128, f32[1280]{0:T(1024)S(1)} %get-tuple-element.129, ...), kind=kLoop, calls=%fused_computation.63 | loop fusion | flops 44564480 | bytes 21012480 | tf_op jit(solution)/shard_map/convert_element_type | solution.py:76
  103.8 11.4 %copy.83 = f32[2048,1280]{0,1:T(8,128)} copy(f32[2048,1280]{1,0:T(8,128)} %fusion.47) | data formatting | bytes 20971520 | tf_op jit(solution)/shard_map/convert_element_type | solution.py:76
  115.2 9.2 %copy.101 = f32[160,8,8,256]{3,2,1,0:T(8,128)S(1)} copy(f32[160,8,8,256]{3,1,2,0:T(8,128)} %bitcast.126) | data formatting | bytes 20971520
  127.9 6.1 %copy.85 = bf16[8,256,20,64]{1,3,2,0:T(8,128)(2,1)} copy(bf16[8,256,20,64]{1,0,3,2:T(8,128)(2,1)} %multiply_convert_fusion.4) | data formatting | bytes 10485760
  136.5 307.2 %while.24 = (s32[]{:T(128)}, f32[20,64,128]{2,1,0:T(8,128)S(1)}, f32[8,256,20,64]{1,0,3,2:T(8,128)}, f32[8,256,20]{1,0,2:T(8,128)S(1)}, bf16[8,256,20,64]{1,3,2,...) while((s32[]{:T(128)}, f32[20,64,128]{2,1,0:T(8,128)S(1)}, ...), condition=%wide.region_3.4_spmd.clone, body=%wide.region_0.3_spmd.clone.sunk | while | flops 1199117312 | bytes 13914835 | solution.py:79
  145.1 30.0 %dynamic_update_slice.6 = f32[8,256,20,64]{1,0,3,2:T(8,128)} dynamic-update-slice(f32[8,256,20,64]{1,0,3,2:T(8,128)} %get-tuple-element.251, f32[1,256,20,64]{1,0,3,2:T(1,128)S(1)} %copy.120, s32[]{:T(128)S(6)} %copy.125, s32[]{:T(128)} %constant.36.clone.1..sunk, s32[]{:T(128)} %constant.36.clone.1..sunk, s32[]{:T(128)} %constant.36.clone.1..sunk) | dynamic-update-slice | bytes 2621444 | tf_op jit(solution)/shard_map/while/body/jit(dynamic_update_index_in_dim)/dynamic_update_slice | solution.py:79
  183.5 30.0 %dynamic_update_slice.6 = f32[8,256,20,64]{1,0,3,2:T(8,128)} dynamic-update-slice(f32[8,256,20,64]{1,0,3,2:T(8,128)} %get-tuple-element.251, f32[1,256,20,64]{1,0,3,2:T(1,128)S(1)} %copy.120, s32[]{:T(128)S(6)} %copy.125, s32[]{:T(128)} %constant.36.clone.1..sunk, s32[]{:T(128)} %constant.36.clone.1..sunk, s32[]{:T(128)} %constant.36.clone.1..sunk) | dynamic-update-slice | bytes 2621444 | tf_op jit(solution)/shard_map/while/body/jit(dynamic_update_index_in_dim)/dynamic_update_slice | solution.py:79
  221.9 30.0 %dynamic_update_slice.6 = f32[8,256,20,64]{1,0,3,2:T(8,128)} dynamic-update-slice(f32[8,256,20,64]{1,0,3,2:T(8,128)} %get-tuple-element.251, f32[1,256,20,64]{1,0,3,2:T(1,128)S(1)} %copy.120, s32[]{:T(128)S(6)} %copy.125, s32[]{:T(128)} %constant.36.clone.1..sunk, s32[]{:T(128)} %constant.36.clone.1..sunk, s32[]{:T(128)} %constant.36.clone.1..sunk) | dynamic-update-slice | bytes 2621444 | tf_op jit(solution)/shard_map/while/body/jit(dynamic_update_index_in_dim)/dynamic_update_slice | solution.py:79
  260.2 30.0 %dynamic_update_slice.6 = f32[8,256,20,64]{1,0,3,2:T(8,128)} dynamic-update-slice(f32[8,256,20,64]{1,0,3,2:T(8,128)} %get-tuple-element.251, f32[1,256,20,64]{1,0,3,2:T(1,128)S(1)} %copy.120, s32[]{:T(128)S(6)} %copy.125, s32[]{:T(128)} %constant.36.clone.1..sunk, s32[]{:T(128)} %constant.36.clone.1..sunk, s32[]{:T(128)} %constant.36.clone.1..sunk) | dynamic-update-slice | bytes 2621444 | tf_op jit(solution)/shard_map/while/body/jit(dynamic_update_index_in_dim)/dynamic_update_slice | solution.py:79
  298.6 30.0 %dynamic_update_slice.6 = f32[8,256,20,64]{1,0,3,2:T(8,128)} dynamic-update-slice(f32[8,256,20,64]{1,0,3,2:T(8,128)} %get-tuple-element.251, f32[1,256,20,64]{1,0,3,2:T(1,128)S(1)} %copy.120, s32[]{:T(128)S(6)} %copy.125, s32[]{:T(128)} %constant.36.clone.1..sunk, s32[]{:T(128)} %constant.36.clone.1..sunk, s32[]{:T(128)} %constant.36.clone.1..sunk) | dynamic-update-slice | bytes 2621444 | tf_op jit(solution)/shard_map/while/body/jit(dynamic_update_index_in_dim)/dynamic_update_slice | solution.py:79
  337.0 30.0 %dynamic_update_slice.6 = f32[8,256,20,64]{1,0,3,2:T(8,128)} dynamic-update-slice(f32[8,256,20,64]{1,0,3,2:T(8,128)} %get-tuple-element.251, f32[1,256,20,64]{1,0,3,2:T(1,128)S(1)} %copy.120, s32[]{:T(128)S(6)} %copy.125, s32[]{:T(128)} %constant.36.clone.1..sunk, s32[]{:T(128)} %constant.36.clone.1..sunk, s32[]{:T(128)} %constant.36.clone.1..sunk) | dynamic-update-slice | bytes 2621444 | tf_op jit(solution)/shard_map/while/body/jit(dynamic_update_index_in_dim)/dynamic_update_slice | solution.py:79
  375.3 30.0 %dynamic_update_slice.6 = f32[8,256,20,64]{1,0,3,2:T(8,128)} dynamic-update-slice(f32[8,256,20,64]{1,0,3,2:T(8,128)} %get-tuple-element.251, f32[1,256,20,64]{1,0,3,2:T(1,128)S(1)} %copy.120, s32[]{:T(128)S(6)} %copy.125, s32[]{:T(128)} %constant.36.clone.1..sunk, s32[]{:T(128)} %constant.36.clone.1..sunk, s32[]{:T(128)} %constant.36.clone.1..sunk) | dynamic-update-slice | bytes 2621444 | tf_op jit(solution)/shard_map/while/body/jit(dynamic_update_index_in_dim)/dynamic_update_slice | solution.py:79
  413.7 30.0 %dynamic_update_slice.6 = f32[8,256,20,64]{1,0,3,2:T(8,128)} dynamic-update-slice(f32[8,256,20,64]{1,0,3,2:T(8,128)} %get-tuple-element.251, f32[1,256,20,64]{1,0,3,2:T(1,128)S(1)} %copy.120, s32[]{:T(128)S(6)} %copy.125, s32[]{:T(128)} %constant.36.clone.1..sunk, s32[]{:T(128)} %constant.36.clone.1..sunk, s32[]{:T(128)} %constant.36.clone.1..sunk) | dynamic-update-slice | bytes 2621444 | tf_op jit(solution)/shard_map/while/body/jit(dynamic_update_index_in_dim)/dynamic_update_slice | solution.py:79
  443.7 11.4 %reshape.140 = f32[2048,20,64]{0,2,1:T(8,128)} reshape(f32[8,256,20,64]{1,0,3,2:T(8,128)} %get-tuple-element.65) | data formatting | bytes 20971520 | tf_op jit(solution)/shard_map/reshape | solution.py:100
  455.2 49.0 %while.23 = (s32[]{:T(128)}, f32[20,64,128]{2,1,0:T(8,128)S(1)}, f32[20]{0:T(128)S(1)}, f32[20,64,128]{2,1,0:T(8,128)S(1)}, s32[]{:T(128)}) while((s32[]{:T(128)}, f32[20,64,128]{2,1,0:T(8,128)S(1)}, f32[20]{0:T(128)S(1)}, f32[20,64,128]{2,1,0:T(8,128)S(1)}, s32[]{:T(128)}) %tuple.57), condition=%wide.region_7.8_spmd, body=%wide.region_6.7_spmd.sunk | while | flops 327682 | bytes 4587701 | solution.py:95
  456.8 15.8 %collective-permute-done = f32[20,64,128]{2,1,0:T(8,128)S(1)} collective-permute-done((f32[20,64,128]{2,1,0:T(8,128)S(1)}, f32[20,64,128]{2,1,0:T(8,128)S(1)}, u32[]{:S(2)}, u32[]{:S(2)}) %collective-permute-start) | collective-permute-done | bytes 655392 | tf_op jit(solution)/shard_map/while/body/eval_jaxpr/ppermute | solution.py:13
  474.0 14.9 %collective-permute-done = f32[20,64,128]{2,1,0:T(8,128)S(1)} collective-permute-done((f32[20,64,128]{2,1,0:T(8,128)S(1)}, f32[20,64,128]{2,1,0:T(8,128)S(1)}, u32[]{:S(2)}, u32[]{:S(2)}) %collective-permute-start) | collective-permute-done | bytes 655392 | tf_op jit(solution)/shard_map/while/body/eval_jaxpr/ppermute | solution.py:13
  490.3 13.9 %collective-permute-done = f32[20,64,128]{2,1,0:T(8,128)S(1)} collective-permute-done((f32[20,64,128]{2,1,0:T(8,128)S(1)}, f32[20,64,128]{2,1,0:T(8,128)S(1)}, u32[]{:S(2)}, u32[]{:S(2)}) %collective-permute-start) | collective-permute-done | bytes 655392 | tf_op jit(solution)/shard_map/while/body/eval_jaxpr/ppermute | solution.py:13
  508.5 8.9 %add_convert_fusion = bf16[2048,20,64]{0,2,1:T(8,128)(2,1)} fusion(f32[2048,20,64]{0,2,1:T(8,128)} %bitcast.127, f32[2048,20,64]{0,2,1:T(8,128)S(1)} %copy-done, f32[2048,20,64]{0,2,1:T(8,128)S(1)} %fusion.57, f32[20]{0:T(128)S(1)} %copy-done.6, f32[2048,20]{0,1:T(8,128)S(1)} %bitcast_exponential_fusion.1), kind=kLoop, calls=%fused_computation.59 | loop fusion | flops 13107200 | bytes 36864080 | tf_op jit(solution)/shard_map/convert_element_type | solution.py:104
  517.4 9.5 %all_to_all.44 = bf16[4,512,1280]{1,0,2:T(4,128)(2,1)} reshape(bf16[2048,20,64]{0,2,1:T(8,128)(2,1)} %add_convert_fusion) | data formatting | bytes 10485760 | tf_op jit(solution)/shard_map/all_to_all | solution.py:105
  530.5 65.0 %all_to_all.51 = bf16[4,512,1280]{1,2,0:T(8,128)(2,1)} all-to-all(bf16[4,512,1280]{1,2,0:T(8,128)(2,1)S(1)} %copy.91), channel_id=1, replica_groups=mesh['run'=2,'ctx'=4,'head'=4] {'head'}, dimensions={0} | all-to-all | bytes 10485760 | tf_op jit(solution)/shard_map/all_to_all | solution.py:105
  595.5 7.9 %copy.92 = bf16[512,5120]{1,0:T(8,128)(2,1)} copy(bf16[512,5120]{0,1:T(8,128)(2,1)} %bitcast.130) | data formatting | bytes 10485760 | tf_op jit(solution)/shard_map/all_to_all | solution.py:105
  (234 shorter events, 116.9 us)
Async XLA Ops:
  8.1 9.4 %all-to-all-start = ((bf16[512,4,20]{0,2,1:T(8,128)(2,1)}), bf16[512,4,20]{0,2,1:T(8,128)(2,1)S(1)}, u32[]{:S(2)}, u32[]{:S(2)}) async-start(bf16[512,4,20]{0,2,1:T(8,128)(2,1)} %all_to_all.38), calls=%async_computation | async-start | bytes 196608 | tf_op jit(solution)/shard_map/all_to_all | solution.py:55
  17.5 6.0 copy-start.3
  17.5 6.1 copy-start.5
  17.5 6.1 copy-start.4
  17.5 71.7 %all-to-all-start.1 = ((bf16[512,4,1280]{2,0,1:T(8,128)(2,1)}), bf16[512,4,1280]{2,0,1:T(8,128)(2,1)}, u32[]{:S(2)}, u32[]{:S(2)}) async-start(bf16[512,4,1280]{2,0,1:T(8,128)(2,1)} %bitcast.129), calls=%async_computation.1 | async-start | bytes 10485760 | tf_op jit(solution)/shard_map/all_to_all | solution.py:54
  22.7 54.9 %all-gather.2.cloned.1.call-start = ((), (), s32[]{:S(2)}) async-start(), calls=%async_computation.3 | async-start | bytes 1310720 | tf_op jit(solution)/shard_map/all_gather | solution.py:62
  90.0 5.6 collective-permute-start.1
  135.5 1.0 copy-start.1
  455.2 49.1 %copy-start.2 = (bf16[2048,256]{1,0:T(8,128)(2,1)S(1)}, bf16[2048,256]{1,0:T(8,128)(2,1)}, u32[]{:S(2)}) copy-start(bf16[2048,256]{1,0:T(8,128)(2,1)} %copy-done.1) | copy-start | bytes 3145732
  455.4 17.2 %collective-permute-start = (f32[20,64,128]{2,1,0:T(8,128)S(1)}, f32[20,64,128]{2,1,0:T(8,128)S(1)}, u32[]{:S(2)}, u32[]{:S(2)}) collective-permute-start(f32[20,64,128]{2,1,0:T(8,128)S(1)} %multiply_add_fusion.2), channel_id=1, source_target_pairs={{0,4},{4,8},{8,12},{1,5},{5,9},{9,13},{2,6},{6,10},{10,14},{3,7},{... | collective-permute-start | bytes 1966088 | tf_op jit(solution)/shard_map/while/body/eval_jaxpr/ppermute | solution.py:13
  472.7 16.2 %collective-permute-start = (f32[20,64,128]{2,1,0:T(8,128)S(1)}, f32[20,64,128]{2,1,0:T(8,128)S(1)}, u32[]{:S(2)}, u32[]{:S(2)}) collective-permute-start(f32[20,64,128]{2,1,0:T(8,128)S(1)} %multiply_add_fusion.2), channel_id=1, source_target_pairs={{0,4},{4,8},{8,12},{1,5},{5,9},{9,13},{2,6},{6,10},{10,14},{3,7},{... | collective-permute-start | bytes 1966088 | tf_op jit(solution)/shard_map/while/body/eval_jaxpr/ppermute | solution.py:13
  489.0 15.2 %collective-permute-start = (f32[20,64,128]{2,1,0:T(8,128)S(1)}, f32[20,64,128]{2,1,0:T(8,128)S(1)}, u32[]{:S(2)}, u32[]{:S(2)}) collective-permute-start(f32[20,64,128]{2,1,0:T(8,128)S(1)} %multiply_add_fusion.2), channel_id=1, source_target_pairs={{0,4},{4,8},{8,12},{1,5},{5,9},{9,13},{2,6},{6,10},{10,14},{3,7},{... | collective-permute-start | bytes 1966088 | tf_op jit(solution)/shard_map/while/body/eval_jaxpr/ppermute | solution.py:13
  504.3 4.2 copy-start
  504.3 4.3 copy-start.6
Sparse Core Ops, SparseCore 0:
  25.4 52.2 all-gather.1
where the time goes:
time: 620 us; the launch traced here: 610 us
  local copies, waits for them, and re-layouts  324 us (52%)
  waiting for transfers between devices  102 us (16%)
  blocking collectives  65 us (10%)
  matrix products  49.4 us (8%)
  other arithmetic  40.1 us (6%)
  starting transfers between devices  14.9 us (2%)
  between operations  13.7 us (2%)
    dynamic_update_slice x16, local copies, waits for them, and re-layouts, per_device(): lax.scan(block_terms, start_state, (c_rows.reshape(block_count, SPAN, sta...  251 us
    all_to_all x1, blocking collectives, per_device(): lax.all_to_all(regrouped, 'head', split_axis=0, concat_axis=1, tiled=True)  65 us
    all_gather x1, waiting for transfers between devices, per_device(): state_whole = lax.all_gather(state_inputs, 'head', axis=0, tiled=True)  46.5 us
    ppermute x4, waiting for transfers between devices, from_behind(): return lax.ppermute(value, axis, pairs)  45.4 us
    all_to_all x3, local copies, waits for them, and re-layouts, per_device(): lax.all_to_all(regrouped, 'head', split_axis=0, concat_axis=1, tiled=True)  20.9 us
    dot_general x8, matrix products, block_terms(): jnp.einsum('hts,shp->thp', mixing, u_block, preferred_element_type=jnp.fl...  20.4 us
    dot_general x8, matrix products, block_terms(): jnp.einsum('shp,sn->hpn', scaled, b_block.astype(jnp.float32), precision=...  17.3 us
    unnamed x21, local copies, waits for them, and re-layouts  16.5 us
  transfers between devices with their start and end apart: 7, of which 6 were waited for; matrix products, arithmetic and copies ran while one was open for 3% of the time, Pallas kernels for 0%

commit v1 on v0

v1 whole, which is shorter than its diff:
```python
import functools

import jax
import jax.numpy as jnp
from jax import lax
from jax.experimental import pallas as pl
from jax.experimental.pallas import tpu as pltpu
from jax.sharding import PartitionSpec as P

KERNEL = 4
SPAN = 256
GROUP = 256
LANES = 128
LOG2E = 1.4426950408889634
F32 = jnp.float32
BF16 = jnp.bfloat16
MESH = pl.DeviceIdType.MESH


def dot(a, b):
    return jnp.dot(a, b, preferred_element_type=F32)


def split2(v):
    hi = v.astype(BF16)
    lo = (v - hi.astype(F32)).astype(BF16)
    return jnp.concatenate([hi, lo], axis=1)


def silu(v):
    return v * (0.5 + 0.5 * jnp.tanh(0.5 * v))


def softplus(v):
    return jnp.maximum(v, 0.0) + jnp.log(1.0 + jnp.exp(-jnp.abs(v)))


def kernel(
    n_ctx, n_head, heads, width, pieces,
    x_ref, si_ref, sr_ref, cw_ref, cs_ref, sm_ref, out_ref,
    cwb, smb, eb32, ebs, ebr, edge, sedge, xs,
    cum, cum_t, step_hl, w_hl, ec_hl, dec_hl, scores, bt, cc,
    xc, acc, s0, dx, s_out, slots, d_slots, qs, rs, ch_in, ch_out, p_out, inc,
    cw_ss, cw_rs, sm_ss, sm_rs, eb_ss, eb_rs, s_ss, s_rs, d_ss, d_rs, ch_ss, ch_rs, p_ss, p_rs,
):
    tokens, channels = x_ref.shape
    blocks = tokens // SPAN
    per = GROUP // width
    state = cc.shape[1]
    run = lax.axis_index("run")
    c = lax.axis_index("ctx")
    me = lax.axis_index("head")
    flat = c * n_head + me
    total = n_ctx * n_head
    nxt = lax.rem(flat + 1, total)
    prv = lax.rem(flat + total - 1, total)
    up = lax.rem(c + 1, n_ctx)
    down = lax.rem(c + n_ctx - 1, n_ctx)

    def peer(i):
        return lax.rem(me + i, n_head)

    def at_head(h):
        return (run, c, h)

    barrier = pltpu.get_barrier_semaphore()
    for i in range(1, n_head):
        pl.semaphore_signal(barrier, inc=1, device_id=at_head(peer(i)), device_id_type=MESH)
    for f in (nxt, prv):
        pl.semaphore_signal(
            barrier, inc=1, device_id=(run, f // n_head, lax.rem(f, n_head)), device_id_type=MESH
        )
    for z in (up, down):
        pl.semaphore_signal(barrier, inc=1, device_id=(run, z, me), device_id_type=MESH)

    part = channels // 5
    tail = x_ref[tokens - 16:, :].astype(F32)
    stail = si_ref[tokens - 16:, :].astype(F32)
    eb32[...] = jnp.zeros_like(eb32)
    for i in range(5):
        eb32[3 * i:3 * i + 3, :] = tail[13:16, i * part:(i + 1) * part]
    for r in range(3):
        eb32[15:16, r * 2 * state:(r + 1) * 2 * state] = stail[13 + r:14 + r, :]
    ebs[...] = eb32[...].astype(BF16)
    cwb[me] = cw_ref[...]
    smb[me] = pltpu.roll(sm_ref[...], me * (heads // n_head), 1)

    pl.semaphore_wait(barrier, n_head - 1 + 4)

    edge_copy = pltpu.make_async_remote_copy(
        ebs, ebr, eb_ss, eb_rs, device_id=(run, nxt // n_head, lax.rem(nxt, n_head)), device_id_type=MESH
    )
    edge_copy.start()

    def param_copies(dst, slot, k):
        return (
            pltpu.make_async_remote_copy(
                smb.at[slot], smb.at[slot], sm_ss.at[k], sm_rs.at[slot],
                device_id=at_head(dst), device_id_type=MESH),
            pltpu.make_async_remote_copy(
                cwb.at[slot], cwb.at[slot], cw_ss.at[k], cw_rs.at[slot],
                device_id=at_head(dst), device_id_type=MESH),
        )

    for i in range(1, n_head):
        for copy in param_copies(peer(i), me, i):
            copy.start()
    for i in range(1, n_head):
        param_copies(peer(i), peer(i), i)[0].wait_recv()

    small = jnp.sum(smb[...], axis=0)
    bias = small[0:1]
    rate = jnp.exp(small[1:2])
    gain = small[2:3]
    raw = jnp.concatenate(
        [sr_ref[...].astype(F32), jnp.zeros((tokens, LANES - heads), F32)], axis=1
    )
    step = softplus(raw + bias)
    decay = -step * rate
    rows = lax.broadcasted_iota(jnp.int32, (SPAN, SPAN), 0)
    cols = lax.broadcasted_iota(jnp.int32, (SPAN, SPAN), 1)
    lower = rows >= cols
    tri = jnp.where(lower, 1.0, 0.0).astype(F32)
    step_hl[...] = split2(step)
    ends = []
    for b in range(blocks):
        lo = b * SPAN
        cm = jnp.dot(tri, decay[lo:lo + SPAN] * LOG2E, precision=lax.Precision.HIGHEST,
                     preferred_element_type=F32)
        cum[lo:lo + SPAN, :] = cm
        cum_t[:, lo:lo + SPAN] = cm.T
        end = cm[SPAN - 1:SPAN]
        w_hl[lo:lo + SPAN, :] = split2(jnp.exp2(end - cm))
        ec_hl[lo:lo + SPAN, :] = split2(jnp.exp2(cm))
        ends.append(end)
    dec_rows = jnp.concatenate(
        [jnp.exp2(ends[0]), jnp.exp2(ends[1]), jnp.exp2(ends[0] + ends[1]), gain,
         jnp.zeros((12, LANES), F32)], axis=0)
    dec_hl[...] = split2(dec_rows)

    edge_copy.wait_recv()
    eb32[...] = jnp.where(flat == 0, 0.0, ebr[...].astype(F32))
    for i in range(5):
        edge[5:8, i * part:(i + 1) * part] = eb32[3 * i:3 * i + 3, :]
    for r in range(3):
        sedge[5 + r:6 + r, :] = eb32[15:16, r * 2 * state:(r + 1) * 2 * state]

    def conv(l, taps):
        v = taps(KERNEL) + taps(0) * xs[l, pl.ds(8 - KERNEL + 1, tokens), :]
        for k in range(1, KERNEL):
            v = v + taps(k) * xs[l, pl.ds(8 - KERNEL + 1 + k, tokens), :]
        return silu(v).astype(BF16)

    for l in range(2):
        at = pl.ds(l * LANES, LANES)
        xs[l, 0:8, :] = sedge[:, at]
        xs[l, 8:8 + tokens, :] = si_ref[:, at].astype(F32)
    b_conv = conv(0, lambda k: cs_ref[k:k + 1, 0:LANES])
    c_conv = conv(1, lambda k: cs_ref[k:k + 1, LANES:2 * LANES])
    b_t = b_conv.astype(F32).T.astype(BF16)
    bt[...] = b_t
    cc[...] = c_conv
    for b in range(blocks):
        lo = b * SPAN
        sc = dot(c_conv[lo:lo + SPAN], b_t[:, lo:lo + SPAN])
        scores[b] = jnp.where(lower, sc, 0.0)

    for i in range(1, n_head):
        param_copies(peer(i), peer(i), i)[1].wait_recv()

    def spreader(g):
        k = lax.broadcasted_iota(jnp.int32, (2 * LANES, GROUP), 0)
        l = lax.broadcasted_iota(jnp.int32, (2 * LANES, GROUP), 1)
        return jnp.where(lax.rem(k, LANES) == g * per + l // width, 1.0, 0.0).astype(BF16)

    def state_copies(dst, slot, k, j):
        return (
            pltpu.make_async_remote_copy(
                s_out.at[dst, j], slots.at[slot, j], s_ss.at[k, j], s_rs.at[slot, j],
                device_id=at_head(dst), device_id_type=MESH),
            pltpu.make_async_remote_copy(
                dx.at[dst, j], d_slots.at[slot, j], d_ss.at[k, j], d_rs.at[slot, j],
                device_id=at_head(dst), device_id_type=MESH),
        )

    def form(q, j):
        g = q * pieces + j
        base = pl.multiple_of(g * GROUP, GROUP)
        jb = pl.multiple_of(j * GROUP, GROUP)
        spread = spreader(g)
        us = []
        sb = dot(step_hl[...], spread)
        wb = dot(w_hl[...], spread)
        for l in range(2):
            at = pl.ds(pl.multiple_of(base + l * LANES, LANES), LANES)
            tap_at = pl.ds(pl.multiple_of(jb + l * LANES, LANES), LANES)
            xs[l, 0:8, :] = edge[:, at]
            xs[l, 8:8 + tokens, :] = x_ref[:, at].astype(F32)
            xv = conv(l, lambda k: cwb[q, k:k + 1, tap_at])
            xc[:, at] = xv
            half = slice(l * LANES, (l + 1) * LANES)
            u = (xv.astype(F32) * sb[:, half]).astype(BF16)
            us.append((u.astype(F32) * wb[:, half]).astype(BF16))
        uw = jnp.concatenate(us, axis=1)
        d = dot(dec_hl[...], spread)[0:8]
        dx[q, j] = d
        first = dot(bt[:, 0:SPAN], uw[0:SPAN])
        second = dot(bt[:, SPAN:2 * SPAN], uw[SPAN:2 * SPAN])
        s0[q, j] = first
        s_out[q, j] = (d[1:2] * first + second).astype(BF16)

    def form_piece(j, carry):
        def far(i, carry2):
            q = peer(i)
            form(q, j)
            for copy in state_copies(q, me, i, j):
                copy.start()
            return carry2

        lax.fori_loop(1, n_head, far, 0)
        form(me, j)
        slots[me, j] = s_out[me, j]
        d_slots[me, j] = dx[me, j]
        return carry

    lax.fori_loop(0, pieces, form_piece, 0)

    lane = lax.broadcasted_iota(jnp.int32, (1, LANES), 1)

    def local(g, b):
        lo = b * SPAN
        half = SPAN // 2
        base = pl.multiple_of(g * GROUP, GROUP)
        q = g // pieces
        j = lax.rem(g, pieces)
        spread = spreader(g)
        sb = dot(step_hl[lo:lo + SPAN, :], spread)
        turned = pltpu.roll(cum[lo:lo + SPAN, :], lax.rem(LANES - g * per, LANES), 1)
        top_scores = scores[b, 0:half, 0:half]
        low_scores = scores[b, half:SPAN, :]
        for l in range(2):
            at = pl.ds(pl.multiple_of(base + l * LANES, LANES), LANES)
            xv = xc[lo:lo + SPAN, at].astype(F32)
            u = (xv * sb[:, l * LANES:(l + 1) * LANES]).astype(BF16)
            tops, lows = [], []
            for k in range(2):
                h = l * 2 + k
                col = turned[:, h:h + 1]
                row = cum_t[pl.ds(g * per + h, 1), lo:lo + SPAN]
                top = jnp.exp2(jnp.minimum(col[0:half] - row[:, 0:half], 0.0)) * top_scores
                low = jnp.exp2(jnp.minimum(col[half:SPAN] - row, 0.0)) * low_scores
                tops.append(dot(top.astype(BF16), u[0:half]))
                lows.append(dot(low.astype(BF16), u))
            skip = dx[q, j, 3:4, l * LANES:(l + 1) * LANES]
            acc[lo:lo + half, at] = (
                jnp.where(lane < width, tops[0], tops[1]) + skip * xv[0:half])
            acc[lo + half:lo + SPAN, at] = (
                jnp.where(lane < width, lows[0], lows[1]) + skip * xv[half:SPAN])

    def local_all(b):
        def body(g, carry):
            local(g, b)
            return carry
        lax.fori_loop(0, n_head * pieces, body, 0)

    local_all(0)

    def chain_copy(j):
        return pltpu.make_async_remote_copy(
            ch_out.at[j], ch_in.at[j], ch_ss.at[j], ch_rs.at[j],
            device_id=(run, up, me), device_id_type=MESH)

    def gather_piece(j, carry):
        for i in range(1, n_head):
            for copy in state_copies(peer(i), peer(i), i, j):
                copy.wait_recv()
        q_sum = slots[0, j].astype(F32)
        r = d_slots[0, j, 2:3]
        for e in range(1, n_head):
            d = d_slots[e, j, 2:3]
            q_sum = d * q_sum + slots[e, j].astype(F32)
            r = d * r
        qs[j] = q_sum
        rs[j] = jnp.broadcast_to(r, (8, GROUP))
        return carry

    lax.fori_loop(0, pieces, gather_piece, 0)

    def back_copy(dst, slot, k, j):
        return pltpu.make_async_remote_copy(
            p_out.at[dst, j], inc.at[slot, j], p_ss.at[k, j], p_rs.at[slot, j],
            device_id=at_head(dst), device_id_type=MESH)

    def chain_piece(j, carry):
        @pl.when(c > 0)
        def _():
            chain_copy(j).wait_recv()

        @pl.when(c == 0)
        def _():
            ch_in[j] = jnp.zeros((state, GROUP), BF16)

        arriving = ch_in[j].astype(F32)

        @pl.when(c < n_ctx - 1)
        def _():
            ch_out[j] = (rs[j, 0:1] * arriving + qs[j]).astype(BF16)
            chain_copy(j).start()

        prefix = arriving
        p_out[0, j] = prefix.astype(BF16)
        for e in range(1, n_head):
            prefix = d_slots[e - 1, j, 2:3] * prefix + slots[e - 1, j].astype(F32)
            p_out[e, j] = prefix.astype(BF16)
        for i in range(1, n_head):
            back_copy(peer(i), me, i, j).start()
        inc[me, j] = p_out[me, j]
        return carry

    lax.fori_loop(0, pieces, chain_piece, 0)

    local_all(1)

    def finish(q, j):
        g = q * pieces + j
        base = pl.multiple_of(g * GROUP, GROUP)
        spread = spreader(g)
        entering = inc[q, j]
        middle = (dx[q, j, 0:1] * entering.astype(F32) + s0[q, j]).astype(BF16)
        eb = dot(ec_hl[...], spread)
        at = pl.ds(base, GROUP)
        out_ref[0:SPAN, at] = (
            acc[0:SPAN, at] + eb[0:SPAN] * dot(cc[0:SPAN, :], entering)).astype(BF16)
        out_ref[SPAN:2 * SPAN, at] = (
            acc[SPAN:2 * SPAN, at] + eb[SPAN:2 * SPAN] * dot(cc[SPAN:2 * SPAN, :], middle)
        ).astype(BF16)

    def finish_piece(j, carry):
        finish(me, j)

        def far(i, carry2):
            q = peer(i)
            back_copy(q, q, i, j).wait_recv()
            finish(q, j)
            return carry2

        return lax.fori_loop(1, n_head, far, carry)

    lax.fori_loop(0, pieces, finish_piece, 0)

    edge_copy.wait_send()
    for i in range(1, n_head):
        for copy in param_copies(peer(i), me, i):
            copy.wait_send()

    def drain(j, carry):
        for i in range(1, n_head):
            for copy in state_copies(peer(i), me, i, j):
                copy.wait_send()
            back_copy(peer(i), me, i, j).wait_send()

        @pl.when(c < n_ctx - 1)
        def _():
            chain_copy(j).wait_send()
        return carry

    lax.fori_loop(0, pieces, drain, 0)


def per_device(n_ctx, n_head, inner_tokens, state_inputs, step_raw, conv_inner, conv_state, head_rates, skip_gain):
    tokens, channels = inner_tokens.shape
    heads = step_raw.shape[1]
    width = channels // heads
    state = state_inputs.shape[1] // 2
    pieces = channels // n_head // GROUP
    taps = conv_inner.shape[0]
    cw = jnp.pad(conv_inner, ((0, 8 - taps), (0, 0)))
    small = jnp.concatenate([head_rates, skip_gain[None]], axis=0)
    small = jnp.pad(small, ((0, 8 - small.shape[0]), (0, LANES - small.shape[1])))
    part = channels // n_head
    vm = pltpu.VMEM
    dma = pltpu.SemaphoreType.DMA
    grid4 = (n_head, pieces, state, GROUP)
    scratch = [
        vm((n_head, 8, part), F32), vm((n_head, 8, LANES), F32),
        vm((16, channels // 5), F32), vm((16, channels // 5), BF16), vm((16, channels // 5), BF16),
        vm((8, channels), F32), vm((8, 2 * state), F32), vm((2, tokens + 8, LANES), F32),
        vm((tokens, LANES), F32), vm((LANES, tokens), F32),
        vm((tokens, 2 * LANES), BF16), vm((tokens, 2 * LANES), BF16), vm((tokens, 2 * LANES), BF16),
        vm((16, 2 * LANES), BF16),
        vm((tokens // SPAN, SPAN, SPAN), F32), vm((state, tokens), BF16), vm((tokens, state), BF16),
        vm((tokens, channels), BF16), vm((tokens, channels), F32),
        vm(grid4, F32), vm((n_head, pieces, 8, GROUP), F32),
        vm(grid4, BF16), vm(grid4, BF16), vm((n_head, pieces, 8, GROUP), F32),
        vm((pieces, state, GROUP), F32), vm((pieces, 8, GROUP), F32),
        vm((pieces, state, GROUP), BF16), vm((pieces, state, GROUP), BF16),
        vm(grid4, BF16), vm(grid4, BF16),
        dma((n_head,)), dma((n_head,)), dma((n_head,)), dma((n_head,)),
        dma, dma,
        dma((n_head, pieces)), dma((n_head, pieces)), dma((n_head, pieces)), dma((n_head, pieces)),
        dma((pieces,)), dma((pieces,)),
        dma((n_head, pieces)), dma((n_head, pieces)),
    ]
    return pl.pallas_call(
        functools.partial(kernel, n_ctx, n_head, heads, width, pieces),
        out_shape=jax.ShapeDtypeStruct((tokens, channels), BF16),
        in_specs=[pl.BlockSpec(memory_space=pltpu.VMEM)] * 6,
        out_specs=pl.BlockSpec(memory_space=pltpu.VMEM),
        scratch_shapes=scratch,
        compiler_params=pltpu.CompilerParams(
            collective_id=0, has_side_effects=True, vmem_limit_bytes=60 * 1024 * 1024
        ),
        name="ssd_layer",
    )(inner_tokens, state_inputs, step_raw, cw, conv_state, small)


def solution(mesh):
    return jax.shard_map(
        functools.partial(per_device, mesh.shape["ctx"], mesh.shape["head"]),
        mesh=mesh,
        in_specs=(
            P(("run", "ctx", "head"), None),
            P(("run", "ctx", "head"), None),
            P(("run", "ctx", "head"), None),
            P(None, "head"),
            P(),
            P("run", "head"),
            P("head"),
        ),
        out_specs=P(("run", "ctx", "head"), None),
        check_vma=False,
    )
```

time: 620 us -> 79.2 us (0.13); the launches traced: 610 us -> 78.2 us
  local copies, waits for them, and re-layouts: 324 us -> 8.22 us
  waiting for transfers between devices: 102 us -> 0 us
  Pallas kernels: 0 us -> 68.7 us
  blocking collectives: 65 us -> 0 us
  matrix products: 49.4 us -> 0 us
  other arithmetic: 40.1 us -> 1.3 us
  starting transfers between devices: 14.9 us -> 0 us
  between operations: 13.7 us -> 0.01 us
    dynamic_update_slice x16 -> x0, local copies, waits for them, and re-layouts: 251 us -> none  [per_device(): lax.scan(block_terms, start_state, (c_rows.reshape(block_count, SPAN, sta...]
    pallas_call x0 -> x1, Pallas kernels: none -> 68.7 us  [per_device(): pl.pallas_call(functools.partial(kernel, n_ctx, n_head, heads, width, pie...]
    all_to_all x1 -> x0, blocking collectives: 65 us -> none  [per_device(): lax.all_to_all(regrouped, 'head', split_axis=0, concat_axis=1, tiled=True)]
    dot_general x33 -> x0, matrix products: 49.4 us -> none  [the longest x8 20.4 us: block_terms(): jnp.einsum('hts,shp->thp', mixing, u_block, preferred_element_type=jnp.fl...]
    all_gather x1 -> x0, waiting for transfers between devices: 46.5 us -> none  [per_device(): state_whole = lax.all_gather(state_inputs, 'head', axis=0, tiled=True)]
    ppermute x4 -> x0, waiting for transfers between devices: 45.4 us -> none  [from_behind(): return lax.ppermute(value, axis, pairs)]
    all_to_all x5 -> x0, local copies, waits for them, and re-layouts: 27.6 us -> none  [the longest x3 20.9 us: per_device(): lax.all_to_all(regrouped, 'head', split_axis=0, concat_axis=1, tiled=True)]
    convert_element_type x9 -> x0, other arithmetic: 26.8 us -> none  [the longest x1 8.9 us: per_device(): regrouped = summed.astype(jnp.bfloat16).reshape(context, channels)]
  transfers between devices with their start and end apart: 7 -> 0, of which waited for: 6 -> 0; matrix products, arithmetic and copies ran while one was open for 3% -> 0% of each run, Pallas kernels for 0% -> 0%
where the time goes in v1:
time: 79.2 us; the launch traced here: 78.2 us
  Pallas kernels  68.7 us (87%)
  local copies, waits for them, and re-layouts  8.22 us (10%)
  other arithmetic  1.3 us (2%)
    pallas_call x1, Pallas kernels, per_device(): pl.pallas_call(functools.partial(kernel, n_ctx, n_head, heads, width, pie...  68.7 us
    unnamed x2, local copies, waits for them, and re-layouts  6.83 us

profile of v1, /device:TPU:28, one launch (start us, length us, event | category | flops | bytes accessed | tf_op | source)
XLA Modules:
  0.0 78.2 jit_solution(13431879629241472275)
XLA Ops:
  0.0 1.3 %select_maximum_fusion.sm_ref = f32[8,128]{1,0:T(8,128)} fusion(f32[1,20]{1,0:T(1,128)} %bitcast.1, f32[2,20]{1,0:T(2,128)} %param.12), kind=kLoop, calls=%fused_computation | loop fusion | flops 8192 | bytes 4336 | tf_op jit(solution)/shard_map/concatenate | solution.py:378
  1.3 1.4 %pad.8.cw_ref = f32[8,1280]{1,0:T(8,128)} pad(f32[5,1280]{1,0:T(8,128)} %param.10, f32[]{:T(128)} %constant.2.clone.1), padding=0_3x0_0 | pad | bytes 66564 | tf_op jit(solution)/shard_map/jit(_pad)/pad | solution.py:377
  2.7 1.6 %copy.8.sr_ref = bf16[512,80]{1,0:T(8,128)(2,1)} copy(bf16[512,80]{0,1:T(8,128)(2,1)} %param.9) | data formatting | bytes 163840 | tf_op args[2]
  4.3 68.7 %ssd_layer.1 = bf16[512,5120]{1,0:T(8,128)(2,1)} custom-call(bf16[512,5120]{1,0:T(8,128)(2,1)} %x_ref.1, bf16[512,256]{1,0:T(8,128)(2,1)} %si_ref.1, bf16[512,80]{1,0:T(8,128)(2,1)} %copy.8.sr_ref, f32[8,1280]{1,0:T(8,128)} %pad.8.cw_ref, f32[5,256]{1,0:T(8,128)} %cs_ref.1, f32[8,128]{1,0:T(8,128)} %select_maximum_fusion.sm_ref), custom_call_target="tpu_custom_call" | custom-call | tf_op jit(solution)/shard_map/ssd_layer/pallas_call | solution.py:404
  73.0 5.2 %copy.10 = bf16[512,5120]{1,0:T(8,128)(2,1)} copy(bf16[512,5120]{1,0:T(8,128)(2,1)} %ssd_layer.1) | data formatting | bytes 10485760

commit v2 on v1

v2 whole, which is shorter than its diff:
```python
import functools

import jax
import jax.numpy as jnp
from jax import lax
from jax.experimental import pallas as pl
from jax.experimental.pallas import tpu as pltpu
from jax.sharding import PartitionSpec as P

KERNEL = 4
SPAN = 256
GROUP = 256
LANES = 128
LOG2E = 1.4426950408889634
F32 = jnp.float32
BF16 = jnp.bfloat16
MESH = pl.DeviceIdType.MESH


def dot(a, b):
    return jnp.dot(a, b, preferred_element_type=F32)


def split2(v):
    hi = v.astype(BF16)
    lo = (v - hi.astype(F32)).astype(BF16)
    return jnp.concatenate([hi, lo], axis=1)


def silu(v):
    return v * (0.5 + 0.5 * jnp.tanh(0.5 * v))


def softplus(v):
    return jnp.maximum(v, 0.0) + jnp.log(1.0 + jnp.exp(-jnp.abs(v)))


def kernel(
    n_ctx, n_head, heads, width, pieces,
    x_hbm, si_ref, sr_ref, cw_ref, cs_ref, hr_ref, sg_ref,
    acc_hbm, inc, s0_hbm, dx, ec_hl, cc,
    x_ref, tail_v, cwb, smb, eb32, ebs, ebr, edge, sedge, xs,
    cum, cum_t, step_hl, w_hl, dec_hl, scores, bt,
    xc, uv, acc, s0, s_out, slots, d_slots, ch_in, ch_out, p_out,
    cw_ss, cw_rs, sm_ss, sm_rs, eb_ss, eb_rs, s_ss, s_rs, d_ss, d_rs, ch_ss, ch_rs, p_ss, p_rs,
    x_sem, tail_sem, acc_sem, s0_sem, own_sem,
):
    tokens, channels = x_ref.shape
    blocks = tokens // SPAN
    per = GROUP // width
    state = cc.shape[1]
    run = lax.axis_index("run")
    c = lax.axis_index("ctx")
    me = lax.axis_index("head")
    flat = c * n_head + me
    total = n_ctx * n_head
    nxt = lax.rem(flat + 1, total)
    prv = lax.rem(flat + total - 1, total)
    up = lax.rem(c + 1, n_ctx)
    down = lax.rem(c + n_ctx - 1, n_ctx)

    def peer(i):
        return lax.rem(me + i, n_head)

    def at_head(h):
        return (run, c, h)

    def x_copy(q):
        at = pl.ds(pl.multiple_of(q * pieces * GROUP, GROUP), pieces * GROUP)
        return pltpu.make_async_copy(x_hbm.at[:, at], x_ref.at[:, at], x_sem.at[q])

    tail_copy = pltpu.make_async_copy(x_hbm.at[pl.ds(tokens - 16, 16)], tail_v, tail_sem)
    tail_copy.start()
    for q in range(n_head):
        x_copy(q).start()

    barrier = pltpu.get_barrier_semaphore()
    for i in range(1, n_head):
        pl.semaphore_signal(barrier, inc=1, device_id=at_head(peer(i)), device_id_type=MESH)
    for f in (nxt, prv):
        pl.semaphore_signal(
            barrier, inc=1, device_id=(run, f // n_head, lax.rem(f, n_head)), device_id_type=MESH
        )
    for z in (up, down):
        pl.semaphore_signal(barrier, inc=1, device_id=(run, z, me), device_id_type=MESH)

    part = channels // 5
    tail_copy.wait()
    tail = tail_v[...].astype(F32)
    stail = si_ref[tokens - 16:, :].astype(F32)
    eb32[...] = jnp.zeros_like(eb32)
    for i in range(5):
        eb32[3 * i:3 * i + 3, :] = tail[13:16, i * part:(i + 1) * part]
    for r in range(3):
        eb32[15:16, r * 2 * state:(r + 1) * 2 * state] = stail[13 + r:14 + r, :]
    ebs[...] = eb32[...].astype(BF16)
    cwb[me, 0:KERNEL + 1, :] = cw_ref[...]
    cwb[me, KERNEL + 1:8, :] = jnp.zeros((8 - KERNEL - 1, cw_ref.shape[1]), F32)
    own = heads // n_head
    smb[me] = jnp.zeros((8, LANES), F32)
    smb[me, 0:2, 0:own] = hr_ref[...]
    smb[me, 2:3, 0:own] = sg_ref[...]
    smb[me] = pltpu.roll(smb[me], me * own, 1)

    pl.semaphore_wait(barrier, n_head - 1 + 4)

    edge_copy = pltpu.make_async_remote_copy(
        ebs, ebr, eb_ss, eb_rs, device_id=(run, nxt // n_head, lax.rem(nxt, n_head)), device_id_type=MESH
    )
    edge_copy.start()

    def param_copies(dst, slot, k):
        return (
            pltpu.make_async_remote_copy(
                smb.at[slot], smb.at[slot], sm_ss.at[k], sm_rs.at[slot],
                device_id=at_head(dst), device_id_type=MESH),
            pltpu.make_async_remote_copy(
                cwb.at[slot], cwb.at[slot], cw_ss.at[k], cw_rs.at[slot],
                device_id=at_head(dst), device_id_type=MESH),
        )

    for i in range(1, n_head):
        for copy in param_copies(peer(i), me, i):
            copy.start()
    for i in range(1, n_head):
        param_copies(peer(i), peer(i), i)[0].wait_recv()

    small = jnp.sum(smb[...], axis=0)
    bias = small[0:1]
    rate = jnp.exp(small[1:2])
    gain = small[2:3]
    raw = jnp.concatenate(
        [sr_ref[...].astype(F32), jnp.zeros((LANES - heads, tokens), F32)], axis=0
    ).T
    step = softplus(raw + bias)
    decay = -step * rate
    rows = lax.broadcasted_iota(jnp.int32, (SPAN, SPAN), 0)
    cols = lax.broadcasted_iota(jnp.int32, (SPAN, SPAN), 1)
    lower = rows >= cols
    tri = jnp.where(lower, 1.0, 0.0).astype(F32)
    step_hl[...] = split2(step)
    ends = []
    for b in range(blocks):
        lo = b * SPAN
        cm = jnp.dot(tri, decay[lo:lo + SPAN] * LOG2E, precision=lax.Precision.HIGHEST,
                     preferred_element_type=F32)
        cum[lo:lo + SPAN, :] = cm
        cum_t[:, lo:lo + SPAN] = cm.T
        end = cm[SPAN - 1:SPAN]
        w_hl[lo:lo + SPAN, :] = split2(jnp.exp2(end - cm))
        ec_hl[lo:lo + SPAN, :] = split2(jnp.exp2(cm))
        ends.append(end)
    dec_rows = jnp.concatenate(
        [jnp.exp2(ends[0]), jnp.exp2(ends[1]), jnp.exp2(ends[0] + ends[1]), gain,
         jnp.zeros((12, LANES), F32)], axis=0)
    dec_hl[...] = split2(dec_rows)

    edge_copy.wait_recv()
    eb32[...] = jnp.where(flat == 0, 0.0, ebr[...].astype(F32))
    for i in range(5):
        edge[5:8, i * part:(i + 1) * part] = eb32[3 * i:3 * i + 3, :]
    for r in range(3):
        sedge[5 + r:6 + r, :] = eb32[15:16, r * 2 * state:(r + 1) * 2 * state]

    def conv(l, taps):
        v = taps(KERNEL) + taps(0) * xs[l, pl.ds(8 - KERNEL + 1, tokens), :]
        for k in range(1, KERNEL):
            v = v + taps(k) * xs[l, pl.ds(8 - KERNEL + 1 + k, tokens), :]
        return silu(v).astype(BF16)

    for l in range(2):
        at = pl.ds(l * LANES, LANES)
        xs[l, 0:8, :] = sedge[:, at]
        xs[l, 8:8 + tokens, :] = si_ref[:, at].astype(F32)
    b_conv = conv(0, lambda k: cs_ref[k:k + 1, 0:LANES])
    c_conv = conv(1, lambda k: cs_ref[k:k + 1, LANES:2 * LANES])
    b_t = b_conv.astype(F32).T.astype(BF16)
    bt[...] = b_t
    cc[...] = c_conv
    for b in range(blocks):
        lo = b * SPAN
        sc = dot(c_conv[lo:lo + SPAN], b_t[:, lo:lo + SPAN])
        scores[b] = jnp.where(lower, sc, 0.0)

    for i in range(1, n_head):
        param_copies(peer(i), peer(i), i)[1].wait_recv()

    def spreader(g):
        k = lax.broadcasted_iota(jnp.int32, (2 * LANES, GROUP), 0)
        l = lax.broadcasted_iota(jnp.int32, (2 * LANES, GROUP), 1)
        return jnp.where(lax.rem(k, LANES) == g * per + l // width, 1.0, 0.0).astype(BF16)

    def state_copies(dst, slot, k, j):
        return (
            pltpu.make_async_remote_copy(
                s_out.at[dst, j], slots.at[slot, j], s_ss.at[k, j], s_rs.at[slot, j],
                device_id=at_head(dst), device_id_type=MESH),
            pltpu.make_async_remote_copy(
                dx.at[dst, j], d_slots.at[slot, j], d_ss.at[k, j], d_rs.at[slot, j],
                device_id=at_head(dst), device_id_type=MESH),
        )

    def form(q, j, slot):
        g = q * pieces + j
        base = pl.multiple_of(g * GROUP, GROUP)
        jb = pl.multiple_of(j * GROUP, GROUP)
        spread = spreader(g)
        us = []
        sb = dot(step_hl[...], spread)
        wb = dot(w_hl[...], spread)
        for l in range(2):
            at = pl.ds(pl.multiple_of(base + l * LANES, LANES), LANES)
            tap_at = pl.ds(pl.multiple_of(jb + l * LANES, LANES), LANES)
            xs[2 * slot + l, 0:8, :] = edge[:, at]
            xs[2 * slot + l, 8:8 + tokens, :] = x_ref[:, at].astype(F32)
            xv = conv(2 * slot + l, lambda k: cwb[q, k:k + 1, tap_at])
            xc[:, at] = xv
            half = slice(l * LANES, (l + 1) * LANES)
            u = (xv.astype(F32) * sb[:, half]).astype(BF16)
            uv[:, at] = u
            us.append((u.astype(F32) * wb[:, half]).astype(BF16))
        uw = jnp.concatenate(us, axis=1)
        d = dot(dec_hl[...], spread)[0:8]
        dx[q, j] = d
        first = dot(bt[:, 0:SPAN], uw[0:SPAN])
        second = dot(bt[:, SPAN:2 * SPAN], uw[SPAN:2 * SPAN])
        s0[q, j] = first.astype(BF16)
        return d, (d[1:2] * first + second).astype(BF16)

    def send(i, j):
        for copy in state_copies(peer(i), me, i, j):
            copy.start()

    def form_piece(j):
        made = [form(peer(i), j, i % 2) for i in (1, 2)]
        for i in (1, 2):
            s_out[peer(i), j] = made[i - 1][1]
        for i in (1, 2):
            send(i, j)
        far = [form(peer(i), j, i % 2) for i in range(3, n_head)]
        d, mine = form(me, j, 0)
        for i in range(3, n_head):
            s_out[peer(i), j] = far[i - 3][1]
        slots[me, j] = mine
        d_slots[me, j] = d
        for i in range(3, n_head):
            send(i, j)

    lane = lax.broadcasted_iota(jnp.int32, (1, LANES), 1)

    def local(g):
        base = pl.multiple_of(g * GROUP, GROUP)
        q = g // pieces
        j = lax.rem(g, pieces)
        half = SPAN // 2
        for b in range(blocks):
            lo = b * SPAN
            turned = pltpu.roll(cum[lo:lo + SPAN, :], lax.rem(LANES - g * per, LANES), 1)
            for l in range(2):
                at = pl.ds(pl.multiple_of(base + l * LANES, LANES), LANES)
                u = uv[lo:lo + SPAN, at]
                tops, lows = [], []
                for k in range(2):
                    h = l * 2 + k
                    col = turned[:, h:h + 1]
                    row = cum_t[pl.ds(g * per + h, 1), lo:lo + SPAN]
                    top = jnp.exp2(jnp.minimum(col[0:half] - row[:, 0:half], 0.0))
                    low = jnp.exp2(jnp.minimum(col[half:SPAN] - row, 0.0))
                    top = (top * scores[b, 0:half, 0:half]).astype(BF16)
                    low = (low * scores[b, half:SPAN, :]).astype(BF16)
                    tops.append(dot(top, u[0:half]))
                    lows.append(dot(low, u))
                skip = dx[q, j, 3:4, l * LANES:(l + 1) * LANES]
                acc[lo:lo + half, at] = (
                    jnp.where(lane < width, tops[0], tops[1])
                    + skip * xc[lo:lo + half, at].astype(F32)).astype(BF16)
                acc[lo + half:lo + SPAN, at] = (
                    jnp.where(lane < width, lows[0], lows[1])
                    + skip * xc[lo + half:lo + SPAN, at].astype(F32)).astype(BF16)
        acc_copy(g).start()

    def acc_copy(g):
        at = pl.ds(pl.multiple_of(g * GROUP, GROUP), GROUP)
        return pltpu.make_async_copy(acc.at[:, at], acc_hbm.at[:, at], acc_sem.at[g])

    def chain_copy(j):
        return pltpu.make_async_remote_copy(
            ch_out.at[j], ch_in.at[j], ch_ss.at[j], ch_rs.at[j],
            device_id=(run, up, me), device_id_type=MESH)

    def back_copy(dst, slot, k, j):
        return pltpu.make_async_remote_copy(
            p_out.at[dst, j], inc.at[slot, j], p_ss.at[k, j], p_rs.at[slot, j],
            device_id=at_head(dst), device_id_type=MESH)

    def own_copy(j):
        return pltpu.make_async_copy(p_out.at[me, j], inc.at[me, j], own_sem.at[j])

    def chain_piece(j):
        for i in range(1, n_head):
            for copy in state_copies(peer(i), peer(i), i, j):
                copy.wait_recv()
        q_sum = slots[0, j].astype(F32)
        r = d_slots[0, j, 2:3]
        for e in range(1, n_head):
            d = d_slots[e, j, 2:3]
            q_sum = d * q_sum + slots[e, j].astype(F32)
            r = d * r

        @pl.when(c > 0)
        def _():
            chain_copy(j).wait_recv()

        @pl.when(c == 0)
        def _():
            ch_in[j] = jnp.zeros((state, GROUP), BF16)

        arriving = ch_in[j].astype(F32)
        ch_out[j] = (r * arriving + q_sum).astype(BF16)

        @pl.when(c < n_ctx - 1)
        def _():
            chain_copy(j).start()

        prefix = arriving
        p_out[0, j] = prefix.astype(BF16)
        for e in range(1, n_head):
            prefix = d_slots[e - 1, j, 2:3] * prefix + slots[e - 1, j].astype(F32)
            p_out[e, j] = prefix.astype(BF16)
        for i in range(1, n_head):
            back_copy(peer(i), me, i, j).start()
        own_copy(j).start()

    units = n_head * pieces
    every = 3
    turns = pieces + (units - 1) // every + 1
    lag = jnp.minimum(c, turns - 1 - pieces)

    def chain_turn(turn):
        p = turn - 1 - lag

        @pl.when(jnp.logical_and(p >= 0, p < pieces))
        def _():
            chain_piece(p)

    for q in range(n_head):
        x_copy(q).wait()

    def form_turn(j, carry):
        form_piece(j)
        chain_turn(j)
        return carry

    lax.fori_loop(0, pieces, form_turn, 0)
    s0_copy = pltpu.make_async_copy(s0, s0_hbm, s0_sem)
    s0_copy.start()

    def local_turn(u, carry):
        local(u)

        @pl.when(lax.rem(u, every) == 0)
        def _():
            chain_turn(pieces + u // every)
        return carry

    lax.fori_loop(0, units, local_turn, 0)

    edge_copy.wait_send()
    for i in range(1, n_head):
        for copy in param_copies(peer(i), me, i):
            copy.wait_send()

    def drain(j, carry):
        for i in range(1, n_head):
            for copy in state_copies(peer(i), me, i, j):
                copy.wait_send()
            back_copy(peer(i), me, i, j).wait_send()

            back_copy(peer(i), peer(i), i, j).wait_recv()
        own_copy(j).wait()

        @pl.when(c < n_ctx - 1)
        def _():
            chain_copy(j).wait_send()
        return carry

    lax.fori_loop(0, pieces, drain, 0)
    s0_copy.wait()

    def drain_acc(g, carry):
        acc_copy(g).wait()
        return carry

    lax.fori_loop(0, units, drain_acc, 0)


def finish(width, acc_ref, inc_ref, s0_ref, dx_ref, ec_ref, cc_ref, out_ref):
    q = pl.program_id(0)
    pieces = inc_ref.shape[1]
    per = GROUP // width
    for j in range(pieces):
        k = lax.broadcasted_iota(jnp.int32, (2 * LANES, GROUP), 0)
        l = lax.broadcasted_iota(jnp.int32, (2 * LANES, GROUP), 1)
        place = (q * pieces + j) * per + l // width
        spread = jnp.where(lax.rem(k, LANES) == place, 1.0, 0.0).astype(BF16)
        entering = inc_ref[0, j]
        middle = (dx_ref[0, j, 0:1] * entering.astype(F32) + s0_ref[0, j].astype(F32)).astype(BF16)
        at = slice(j * GROUP, (j + 1) * GROUP)
        for b, held in enumerate((entering, middle)):
            rows = slice(b * SPAN, (b + 1) * SPAN)
            carried = dot(ec_ref[rows, :], spread) * dot(cc_ref[rows, :], held)
            out_ref[rows, at] = (acc_ref[rows, at].astype(F32) + carried).astype(BF16)


def per_device(n_ctx, n_head, inner_tokens, state_inputs, step_raw, conv_inner, conv_state, head_rates, skip_gain):
    tokens, channels = inner_tokens.shape
    heads = step_raw.shape[1]
    width = channels // heads
    state = state_inputs.shape[1] // 2
    pieces = channels // n_head // GROUP
    part = channels // n_head
    vm = pltpu.VMEM
    dma = pltpu.SemaphoreType.DMA
    grid4 = (n_head, pieces, state, GROUP)
    small4 = (n_head, pieces, 8, GROUP)
    scratch = [
        vm((tokens, channels), BF16), vm((16, channels), BF16),
        vm((n_head, 8, part), F32), vm((n_head, 8, LANES), F32),
        vm((16, channels // 5), F32), vm((16, channels // 5), BF16), vm((16, channels // 5), BF16),
        vm((8, channels), F32), vm((8, 2 * state), F32), vm((4, tokens + 8, LANES), F32),
        vm((tokens, LANES), F32), vm((LANES, tokens), F32),
        vm((tokens, 2 * LANES), BF16), vm((tokens, 2 * LANES), BF16),
        vm((16, 2 * LANES), BF16),
        vm((tokens // SPAN, SPAN, SPAN), F32), vm((state, tokens), BF16),
        vm((tokens, channels), BF16), vm((tokens, channels), BF16), vm((tokens, channels), BF16),
        vm(grid4, BF16), vm(grid4, BF16), vm(grid4, BF16), vm(small4, F32),
        vm((pieces, state, GROUP), BF16), vm((pieces, state, GROUP), BF16),
        vm(grid4, BF16),
        dma((n_head,)), dma((n_head,)), dma((n_head,)), dma((n_head,)),
        dma, dma,
        dma((n_head, pieces)), dma((n_head, pieces)), dma((n_head, pieces)), dma((n_head, pieces)),
        dma((pieces,)), dma((pieces,)),
        dma((n_head, pieces)), dma((n_head, pieces)),
        dma((n_head,)), dma, dma((n_head * pieces,)), dma, dma((pieces,)),
    ]
    in_vmem = pl.BlockSpec(memory_space=pltpu.VMEM)
    anywhere = pl.BlockSpec(memory_space=pl.ANY)
    shape = jax.ShapeDtypeStruct
    parts = pl.pallas_call(
        functools.partial(kernel, n_ctx, n_head, heads, width, pieces),
        out_shape=(
            shape((tokens, channels), BF16), shape(grid4, BF16), shape(grid4, BF16),
            shape(small4, F32), shape((tokens, 2 * LANES), BF16), shape((tokens, state), BF16),
        ),
        in_specs=[anywhere] + [in_vmem] * 6,
        out_specs=(anywhere, anywhere, anywhere, in_vmem, in_vmem, in_vmem),
        scratch_shapes=scratch,
        compiler_params=pltpu.CompilerParams(
            collective_id=0, has_side_effects=True, vmem_limit_bytes=56 * 1024 * 1024
        ),
        name="ssd_layer",
    )(inner_tokens, state_inputs, step_raw.T, conv_inner, conv_state, head_rates, skip_gain[None])
    column = pl.BlockSpec((tokens, part), lambda q: (0, q))
    states = pl.BlockSpec((1, pieces, state, GROUP), lambda q: (q, 0, 0, 0))
    return pl.pallas_call(
        functools.partial(finish, width),
        grid=(n_head,),
        out_shape=shape((tokens, channels), BF16),
        in_specs=[
            column, states, states,
            pl.BlockSpec((1, pieces, 8, GROUP), lambda q: (q, 0, 0, 0)),
            pl.BlockSpec((tokens, 2 * LANES), lambda q: (0, 0)),
            pl.BlockSpec((tokens, state), lambda q: (0, 0)),
        ],
        out_specs=column,
        compiler_params=pltpu.CompilerParams(vmem_limit_bytes=56 * 1024 * 1024),
        name="carried_terms",
    )(*parts)


def solution(mesh):
    return jax.shard_map(
        functools.partial(per_device, mesh.shape["ctx"], mesh.shape["head"]),
        mesh=mesh,
        in_specs=(
            P(("run", "ctx", "head"), None),
            P(("run", "ctx", "head"), None),
            P(("run", "ctx", "head"), None),
            P(None, "head"),
            P(),
            P("run", "head"),
            P("head"),
        ),
        out_specs=P(("run", "ctx", "head"), None),
        check_vma=False,
    )
```

time: 79.2 us -> 66 us (0.83); the launches traced: 78.2 us -> 65.9 us
  local copies, waits for them, and re-layouts: 8.22 us -> 0 us
  Pallas kernels: 68.7 us -> 65.9 us
  other arithmetic: 1.3 us -> 0 us
    pallas_call x1, Pallas kernels: 68.7 us -> 58.1 us  [per_device(): pl.pallas_call(functools.partial(kernel, n_ctx, n_head, heads, width, pie...]
    pallas_call x0 -> x1, Pallas kernels: none -> 7.78 us  [per_device(): pl.pallas_call(functools.partial(finish, width), grid=(n_head,), out_shap...]
    unnamed x2 -> x0, local copies, waits for them, and re-layouts: 6.83 us -> none
    pad x1 -> x0, local copies, waits for them, and re-layouts: 1.4 us -> none  [per_device(): cw = jnp.pad(conv_inner, ((0, 8 - taps), (0, 0)))]
    concatenate x1 -> x0, other arithmetic: 1.3 us -> none  [per_device(): small = jnp.concatenate([head_rates, skip_gain[None]], axis=0)]
where the time goes in v2:
time: 66 us; the launch traced here: 65.9 us
  Pallas kernels  65.9 us (100%)
    pallas_call x1, Pallas kernels, per_device(): pl.pallas_call(functools.partial(kernel, n_ctx, n_head, heads, width, pie...  58.1 us
    pallas_call x1, Pallas kernels, per_device(): pl.pallas_call(functools.partial(finish, width), grid=(n_head,), out_shap...  7.78 us

profile of v2, /device:TPU:28, one launch (start us, length us, event | category | flops | bytes accessed | tf_op | source)
XLA Modules:
  0.0 65.9 jit_solution(78702979799173475)
XLA Ops:
  0.0 58.1 %ssd_layer.1 = (bf16[512,5120]{1,0:T(8,128)(2,1)}, bf16[4,5,128,256]{3,2,1,0:T(8,128)(2,1)}, bf16[4,5,128,256]{3,2,1,0:T(8,128)(2,1)}, f32[4,5,8,256]{3,2,1,0:T(...) custom-call(bf16[512,5120]{1,0:T(8,128)(2,1)} %x_hbm.1, bf16[512,256]{1,0:T(8,128)(2,1)} %si_ref.1, ...), custom_call_target="tpu_custom_call" | custom-call | tf_op jit(solution)/shard_map/ssd_layer/pallas_call | solution.py:449
  58.1 7.8 %carried_terms.1 = bf16[512,5120]{1,0:T(8,128)(2,1)} custom-call(bf16[512,5120]{1,0:T(8,128)(2,1)} %get-tuple-element.11.acc_ref, bf16[4,5,128,256]{3,2,1,0:T(8,128)(2,1)} %get-tuple-element.12.inc_ref, bf16[4,5,128,256]{3,2,1,0:T(8,128)(2,1)} %get-tuple-element.13.s0_ref, f32[4,5,8,256]{3,2,1,0:T(8,128)} %get-tuple-element.14.dx_ref, ...), custom_call_target="tpu_custom_call" | custom-call | tf_op jit(solution)/shard_map/carried_terms/pallas_call | solution.py:465

commit v3 on v2

--- a/solution.py
+++ b/solution.py
@@ -33,6 +33,14 @@
 
 def softplus(v):
     return jnp.maximum(v, 0.0) + jnp.log(1.0 + jnp.exp(-jnp.abs(v)))
+
+
+def spread_matrix(first, width):
+    k = lax.broadcasted_iota(jnp.int32, (LANES, GROUP), 0)
+    l = lax.broadcasted_iota(jnp.int32, (LANES, GROUP), 1)
+    place = k - jnp.right_shift(l, width.bit_length() - 1)
+    once = jnp.where(place == first, 1.0, 0.0).astype(BF16)
+    return jnp.concatenate([once, once], axis=0)
 
 
 def kernel(
@@ -186,9 +194,7 @@
         param_copies(peer(i), peer(i), i)[1].wait_recv()
 
     def spreader(g):
-        k = lax.broadcasted_iota(jnp.int32, (2 * LANES, GROUP), 0)
-        l = lax.broadcasted_iota(jnp.int32, (2 * LANES, GROUP), 1)
-        return jnp.where(lax.rem(k, LANES) == g * per + l // width, 1.0, 0.0).astype(BF16)
+        return spread_matrix(g * per, width)
 
     def state_copies(dst, slot, k, j):
         return (
@@ -259,7 +265,7 @@
             for l in range(2):
                 at = pl.ds(pl.multiple_of(base + l * LANES, LANES), LANES)
                 u = uv[lo:lo + SPAN, at]
-                tops, lows = [], []
+                mixing = []
                 for k in range(2):
                     h = l * 2 + k
                     col = turned[:, h:h + 1]
@@ -268,15 +274,12 @@
                     low = jnp.exp2(jnp.minimum(col[half:SPAN] - row, 0.0))
                     top = (top * scores[b, 0:half, 0:half]).astype(BF16)
                     low = (low * scores[b, half:SPAN, :]).astype(BF16)
-                    tops.append(dot(top, u[0:half]))
-                    lows.append(dot(low, u))
+                    mixing += [jnp.concatenate([top, jnp.zeros_like(top)], axis=1), low]
+                made = dot(jnp.concatenate(mixing, axis=0), u)
+                local_terms = jnp.where(lane < width, made[0:SPAN], made[SPAN:2 * SPAN])
                 skip = dx[q, j, 3:4, l * LANES:(l + 1) * LANES]
-                acc[lo:lo + half, at] = (
-                    jnp.where(lane < width, tops[0], tops[1])
-                    + skip * xc[lo:lo + half, at].astype(F32)).astype(BF16)
-                acc[lo + half:lo + SPAN, at] = (
-                    jnp.where(lane < width, lows[0], lows[1])
-                    + skip * xc[lo + half:lo + SPAN, at].astype(F32)).astype(BF16)
+                acc[lo:lo + SPAN, at] = (
+                    local_terms + skip * xc[lo:lo + SPAN, at].astype(F32)).astype(BF16)
         acc_copy(g).start()
 
     def acc_copy(g):
@@ -399,10 +402,7 @@
     pieces = inc_ref.shape[1]
     per = GROUP // width
     for j in range(pieces):
-        k = lax.broadcasted_iota(jnp.int32, (2 * LANES, GROUP), 0)
-        l = lax.broadcasted_iota(jnp.int32, (2 * LANES, GROUP), 1)
-        place = (q * pieces + j) * per + l // width
-        spread = jnp.where(lax.rem(k, LANES) == place, 1.0, 0.0).astype(BF16)
+        spread = spread_matrix((q * pieces + j) * per, width)
         entering = inc_ref[0, j]
         middle = (dx_ref[0, j, 0:1] * entering.astype(F32) + s0_ref[0, j].astype(F32)).astype(BF16)
         at = slice(j * GROUP, (j + 1) * GROUP)

time: 66 us -> 66.4 us (level)
  no operation moved by 1% of the time
where the time goes in v3:
time: 66.4 us; the launch traced here: 66.2 us
  Pallas kernels  66.2 us (100%)
    pallas_call x1, Pallas kernels, per_device(): pl.pallas_call(functools.partial(kernel, n_ctx, n_head, heads, width, pie...  58.4 us
    pallas_call x1, Pallas kernels, per_device(): pl.pallas_call(functools.partial(finish, width), grid=(n_head,), out_shap...  7.77 us

profile of v3, /device:TPU:28, one launch (start us, length us, event | category | flops | bytes accessed | tf_op | source)
XLA Modules:
  0.0 66.2 jit_solution(13689865196401170034)
XLA Ops:
  0.0 58.4 %ssd_layer.1 = (bf16[512,5120]{1,0:T(8,128)(2,1)}, bf16[4,5,128,256]{3,2,1,0:T(8,128)(2,1)}, bf16[4,5,128,256]{3,2,1,0:T(8,128)(2,1)}, f32[4,5,8,256]{3,2,1,0:T(...) custom-call(bf16[512,5120]{1,0:T(8,128)(2,1)} %x_hbm.1, bf16[512,256]{1,0:T(8,128)(2,1)} %si_ref.1, ...), custom_call_target="tpu_custom_call" | custom-call | tf_op jit(solution)/shard_map/ssd_layer/pallas_call | solution.py:449
  58.4 7.8 %carried_terms.1 = bf16[512,5120]{1,0:T(8,128)(2,1)} custom-call(bf16[512,5120]{1,0:T(8,128)(2,1)} %get-tuple-element.11.acc_ref, bf16[4,5,128,256]{3,2,1,0:T(8,128)(2,1)} %get-tuple-element.12.inc_ref, bf16[4,5,128,256]{3,2,1,0:T(8,128)(2,1)} %get-tuple-element.13.s0_ref, f32[4,5,8,256]{3,2,1,0:T(8,128)} %get-tuple-element.14.dx_ref, ...), custom_call_target="tpu_custom_call" | custom-call | tf_op jit(solution)/shard_map/carried_terms/pallas_call | solution.py:465

commit v4 on v3

--- a/solution.py
+++ b/solution.py
@@ -11,6 +11,7 @@
 SPAN = 256
 GROUP = 256
 LANES = 128
+CHUNK = 64
 LOG2E = 1.4426950408889634
 F32 = jnp.float32
 BF16 = jnp.bfloat16
@@ -49,7 +50,7 @@
     acc_hbm, inc, s0_hbm, dx, ec_hl, cc,
     x_ref, tail_v, cwb, smb, eb32, ebs, ebr, edge, sedge, xs,
     cum, cum_t, step_hl, w_hl, dec_hl, scores, bt,
-    xc, uv, acc, s0, s_out, slots, d_slots, ch_in, ch_out, p_out,
+    xc, uv, uw, mix, acc, s0, s_out, slots, d_slots, ch_in, ch_out, p_out,
     cw_ss, cw_rs, sm_ss, sm_rs, eb_ss, eb_rs, s_ss, s_rs, d_ss, d_rs, ch_ss, ch_rs, p_ss, p_rs,
     x_sem, tail_sem, acc_sem, s0_sem, own_sem,
 ):
@@ -170,18 +171,18 @@
     for r in range(3):
         sedge[5 + r:6 + r, :] = eb32[15:16, r * 2 * state:(r + 1) * 2 * state]
 
-    def conv(l, taps):
-        v = taps(KERNEL) + taps(0) * xs[l, pl.ds(8 - KERNEL + 1, tokens), :]
+    def conv(l, taps, start, count):
+        v = taps(KERNEL) + taps(0) * xs[l, pl.ds(start + 8 - KERNEL + 1, count), :]
         for k in range(1, KERNEL):
-            v = v + taps(k) * xs[l, pl.ds(8 - KERNEL + 1 + k, tokens), :]
-        return silu(v).astype(BF16)
+            v = v + taps(k) * xs[l, pl.ds(start + 8 - KERNEL + 1 + k, count), :]
+        return silu(v)
 
     for l in range(2):
         at = pl.ds(l * LANES, LANES)
         xs[l, 0:8, :] = sedge[:, at]
         xs[l, 8:8 + tokens, :] = si_ref[:, at].astype(F32)
-    b_conv = conv(0, lambda k: cs_ref[k:k + 1, 0:LANES])
-    c_conv = conv(1, lambda k: cs_ref[k:k + 1, LANES:2 * LANES])
+    b_conv = conv(0, lambda k: cs_ref[k:k + 1, 0:LANES], 0, tokens).astype(BF16)
+    c_conv = conv(1, lambda k: cs_ref[k:k + 1, LANES:2 * LANES], 0, tokens).astype(BF16)
     b_t = b_conv.astype(F32).T.astype(BF16)
     bt[...] = b_t
     cc[...] = c_conv
@@ -211,25 +212,28 @@
         base = pl.multiple_of(g * GROUP, GROUP)
         jb = pl.multiple_of(j * GROUP, GROUP)
         spread = spreader(g)
-        us = []
         sb = dot(step_hl[...], spread)
         wb = dot(w_hl[...], spread)
         for l in range(2):
             at = pl.ds(pl.multiple_of(base + l * LANES, LANES), LANES)
             tap_at = pl.ds(pl.multiple_of(jb + l * LANES, LANES), LANES)
+            half = slice(l * LANES, (l + 1) * LANES)
             xs[2 * slot + l, 0:8, :] = edge[:, at]
-            xs[2 * slot + l, 8:8 + tokens, :] = x_ref[:, at].astype(F32)
-            xv = conv(2 * slot + l, lambda k: cwb[q, k:k + 1, tap_at])
-            xc[:, at] = xv
-            half = slice(l * LANES, (l + 1) * LANES)
-            u = (xv.astype(F32) * sb[:, half]).astype(BF16)
-            uv[:, at] = u
-            us.append((u.astype(F32) * wb[:, half]).astype(BF16))
-        uw = jnp.concatenate(us, axis=1)
+            for r in range(0, tokens, CHUNK):
+                xs[2 * slot + l, 8 + r:8 + r + CHUNK, :] = x_ref[r:r + CHUNK, at].astype(F32)
+            taps = [jnp.broadcast_to(cwb[q, k:k + 1, tap_at], (8, LANES)) for k in range(KERNEL + 1)]
+            taps = [jnp.tile(t, (CHUNK // 8, 1)) for t in taps]
+            for r in range(0, tokens, CHUNK):
+                xv = conv(2 * slot + l, lambda k: taps[k], r, CHUNK).astype(BF16)
+                xc[r:r + CHUNK, at] = xv
+                u = (xv.astype(F32) * sb[r:r + CHUNK, half]).astype(BF16)
+                uv[r:r + CHUNK, at] = u
+                uw[slot, r:r + CHUNK, half] = (
+                    u.astype(F32) * wb[r:r + CHUNK, half]).astype(BF16)
         d = dot(dec_hl[...], spread)[0:8]
         dx[q, j] = d
-        first = dot(bt[:, 0:SPAN], uw[0:SPAN])
-        second = dot(bt[:, SPAN:2 * SPAN], uw[SPAN:2 * SPAN])
+        first = dot(bt[:, 0:SPAN], uw[slot, 0:SPAN, :])
+        second = dot(bt[:, SPAN:2 * SPAN], uw[slot, SPAN:2 * SPAN, :])
         s0[q, j] = first.astype(BF16)
         return d, (d[1:2] * first + second).astype(BF16)
 
@@ -258,24 +262,26 @@
         base = pl.multiple_of(g * GROUP, GROUP)
         q = g // pieces
         j = lax.rem(g, pieces)
-        half = SPAN // 2
         for b in range(blocks):
             lo = b * SPAN
             turned = pltpu.roll(cum[lo:lo + SPAN, :], lax.rem(LANES - g * per, LANES), 1)
             for l in range(2):
                 at = pl.ds(pl.multiple_of(base + l * LANES, LANES), LANES)
                 u = uv[lo:lo + SPAN, at]
-                mixing = []
+                spot = 2 * b + l
                 for k in range(2):
                     h = l * 2 + k
-                    col = turned[:, h:h + 1]
                     row = cum_t[pl.ds(g * per + h, 1), lo:lo + SPAN]
-                    top = jnp.exp2(jnp.minimum(col[0:half] - row[:, 0:half], 0.0))
-                    low = jnp.exp2(jnp.minimum(col[half:SPAN] - row, 0.0))
-                    top = (top * scores[b, 0:half, 0:half]).astype(BF16)
-                    low = (low * scores[b, half:SPAN, :]).astype(BF16)
-                    mixing += [jnp.concatenate([top, jnp.zeros_like(top)], axis=1), low]
-                made = dot(jnp.concatenate(mixing, axis=0), u)
+                    for r in range(0, SPAN, CHUNK):
+                        col = jnp.broadcast_to(turned[r:r + CHUNK, h:h + 1], (CHUNK, LANES))
+                        to = slice(k * SPAN + r, k * SPAN + r + CHUNK)
+                        for s in range(0, r + 1, LANES):
+                            gap = col - row[:, s:s + LANES]
+                            if s + LANES > r:
+                                gap = jnp.minimum(gap, 0.0)
+                            mix[spot, to, s:s + LANES] = (
+                                jnp.exp2(gap) * scores[b, r:r + CHUNK, s:s + LANES]).astype(BF16)
+                made = dot(mix[spot], u)
                 local_terms = jnp.where(lane < width, made[0:SPAN], made[SPAN:2 * SPAN])
                 skip = dx[q, j, 3:4, l * LANES:(l + 1) * LANES]
                 acc[lo:lo + SPAN, at] = (
@@ -357,6 +363,10 @@
     lax.fori_loop(0, pieces, form_turn, 0)
     s0_copy = pltpu.make_async_copy(s0, s0_hbm, s0_sem)
     s0_copy.start()
+
+    for spot in range(4):
+        for k in range(2):
+            mix[spot, k * SPAN:k * SPAN + LANES, LANES:] = jnp.zeros((LANES, SPAN - LANES), BF16)
 
     def local_turn(u, carry):
         local(u)
@@ -432,7 +442,8 @@
         vm((tokens, 2 * LANES), BF16), vm((tokens, 2 * LANES), BF16),
         vm((16, 2 * LANES), BF16),
         vm((tokens // SPAN, SPAN, SPAN), F32), vm((state, tokens), BF16),
-        vm((tokens, channels), BF16), vm((tokens, channels), BF16), vm((tokens, channels), BF16),
+        vm((tokens, channels), BF16), vm((tokens, channels), BF16),
+        vm((2, tokens, GROUP), BF16), vm((4, 2 * SPAN, SPAN), BF16), vm((tokens, channels), BF16),
         vm(grid4, BF16), vm(grid4, BF16), vm(grid4, BF16), vm(small4, F32),
         vm((pieces, state, GROUP), BF16), vm((pieces, state, GROUP), BF16),
         vm(grid4, BF16),

time: 66.4 us -> 67.4 us (1.015)
  no operation moved by 1% of the time
where the time goes in v4:
time: 67.4 us; the launch traced here: 66.8 us
  Pallas kernels  66.8 us (99%)
    pallas_call x1, Pallas kernels, per_device(): pl.pallas_call(functools.partial(kernel, n_ctx, n_head, heads, width, pie...  59.1 us
    pallas_call x1, Pallas kernels, per_device(): pl.pallas_call(functools.partial(finish, width), grid=(n_head,), out_shap...  7.78 us

profile of v4, /device:TPU:28, one launch (start us, length us, event | category | flops | bytes accessed | tf_op | source)
XLA Modules:
  0.0 66.8 jit_solution(5610418407887573815)
XLA Ops:
  0.0 59.1 %ssd_layer.1 = (bf16[512,5120]{1,0:T(8,128)(2,1)}, bf16[4,5,128,256]{3,2,1,0:T(8,128)(2,1)}, bf16[4,5,128,256]{3,2,1,0:T(8,128)(2,1)}, f32[4,5,8,256]{3,2,1,0:T(...) custom-call(bf16[512,5120]{1,0:T(8,128)(2,1)} %x_hbm.1, bf16[512,256]{1,0:T(8,128)(2,1)} %si_ref.1, ...), custom_call_target="tpu_custom_call" | custom-call | tf_op jit(solution)/shard_map/ssd_layer/pallas_call | solution.py:460
  59.1 7.8 %carried_terms.1 = bf16[512,5120]{1,0:T(8,128)(2,1)} custom-call(bf16[512,5120]{1,0:T(8,128)(2,1)} %get-tuple-element.11.acc_ref, bf16[4,5,128,256]{3,2,1,0:T(8,128)(2,1)} %get-tuple-element.12.inc_ref, bf16[4,5,128,256]{3,2,1,0:T(8,128)(2,1)} %get-tuple-element.13.s0_ref, f32[4,5,8,256]{3,2,1,0:T(8,128)} %get-tuple-element.14.dx_ref, ...), custom_call_target="tpu_custom_call" | custom-call | tf_op jit(solution)/shard_map/carried_terms/pallas_call | solution.py:476

commit v5 on v3

--- a/solution.py
+++ b/solution.py
@@ -162,6 +162,15 @@
         [jnp.exp2(ends[0]), jnp.exp2(ends[1]), jnp.exp2(ends[0] + ends[1]), gain,
          jnp.zeros((12, LANES), F32)], axis=0)
     dec_hl[...] = split2(dec_rows)
+    d_slots[me] = split2(dec_rows)
+
+    def decay_copy(dst, slot, k):
+        return pltpu.make_async_remote_copy(
+            d_slots.at[slot], d_slots.at[slot], d_ss.at[k], d_rs.at[slot],
+            device_id=at_head(dst), device_id_type=MESH)
+
+    for i in range(1, n_head):
+        decay_copy(peer(i), me, i).start()
 
     edge_copy.wait_recv()
     eb32[...] = jnp.where(flat == 0, 0.0, ebr[...].astype(F32))
@@ -196,15 +205,10 @@
     def spreader(g):
         return spread_matrix(g * per, width)
 
-    def state_copies(dst, slot, k, j):
-        return (
-            pltpu.make_async_remote_copy(
-                s_out.at[dst, j], slots.at[slot, j], s_ss.at[k, j], s_rs.at[slot, j],
-                device_id=at_head(dst), device_id_type=MESH),
-            pltpu.make_async_remote_copy(
-                dx.at[dst, j], d_slots.at[slot, j], d_ss.at[k, j], d_rs.at[slot, j],
-                device_id=at_head(dst), device_id_type=MESH),
-        )
+    def state_copy(dst, slot, k, j):
+        return pltpu.make_async_remote_copy(
+            s_out.at[dst, j], slots.at[slot, j], s_ss.at[k, j], s_rs.at[slot, j],
+            device_id=at_head(dst), device_id_type=MESH)
 
     def form(q, j, slot):
         g = q * pieces + j
@@ -234,8 +238,7 @@
         return d, (d[1:2] * first + second).astype(BF16)
 
     def send(i, j):
-        for copy in state_copies(peer(i), me, i, j):
-            copy.start()
+        state_copy(peer(i), me, i, j).start()
 
     def form_piece(j):
         made = [form(peer(i), j, i % 2) for i in (1, 2)]
@@ -244,11 +247,10 @@
         for i in (1, 2):
             send(i, j)
         far = [form(peer(i), j, i % 2) for i in range(3, n_head)]
-        d, mine = form(me, j, 0)
+        mine = form(me, j, 0)[1]
         for i in range(3, n_head):
             s_out[peer(i), j] = far[i - 3][1]
         slots[me, j] = mine
-        d_slots[me, j] = d
         for i in range(3, n_head):
             send(i, j)
 
@@ -301,14 +303,14 @@
 
     def chain_piece(j):
         for i in range(1, n_head):
-            for copy in state_copies(peer(i), peer(i), i, j):
-                copy.wait_recv()
+            state_copy(peer(i), peer(i), i, j).wait_recv()
+        spread = spreader(me * pieces + j)
+        ds = [dot(d_slots[e], spread)[2:3] for e in range(n_head)]
         q_sum = slots[0, j].astype(F32)
-        r = d_slots[0, j, 2:3]
+        r = ds[0]
         for e in range(1, n_head):
-            d = d_slots[e, j, 2:3]
-            q_sum = d * q_sum + slots[e, j].astype(F32)
-            r = d * r
+            q_sum = ds[e] * q_sum + slots[e, j].astype(F32)
+            r = ds[e] * r
 
         @pl.when(c > 0)
         def _():
@@ -328,16 +330,16 @@
         prefix = arriving
         p_out[0, j] = prefix.astype(BF16)
         for e in range(1, n_head):
-            prefix = d_slots[e - 1, j, 2:3] * prefix + slots[e - 1, j].astype(F32)
+            prefix = ds[e - 1] * prefix + slots[e - 1, j].astype(F32)
             p_out[e, j] = prefix.astype(BF16)
         for i in range(1, n_head):
             back_copy(peer(i), me, i, j).start()
         own_copy(j).start()
 
     units = n_head * pieces
-    every = 3
+    every = 2
     turns = pieces + (units - 1) // every + 1
-    lag = jnp.minimum(c, turns - 1 - pieces)
+    lag = jnp.minimum(c + 3, turns - 1 - pieces)
 
     def chain_turn(turn):
         p = turn - 1 - lag
@@ -348,6 +350,8 @@
 
     for q in range(n_head):
         x_copy(q).wait()
+    for i in range(1, n_head):
+        decay_copy(peer(i), peer(i), i).wait_recv()
 
     def form_turn(j, carry):
         form_piece(j)
@@ -373,10 +377,12 @@
         for copy in param_copies(peer(i), me, i):
             copy.wait_send()
 
+    for i in range(1, n_head):
+        decay_copy(peer(i), me, i).wait_send()
+
     def drain(j, carry):
         for i in range(1, n_head):
-            for copy in state_copies(peer(i), me, i, j):
-                copy.wait_send()
+            state_copy(peer(i), me, i, j).wait_send()
             back_copy(peer(i), me, i, j).wait_send()
 
             back_copy(peer(i), peer(i), i, j).wait_recv()
@@ -433,12 +439,12 @@
         vm((16, 2 * LANES), BF16),
         vm((tokens // SPAN, SPAN, SPAN), F32), vm((state, tokens), BF16),
         vm((tokens, channels), BF16), vm((tokens, channels), BF16), vm((tokens, channels), BF16),
-        vm(grid4, BF16), vm(grid4, BF16), vm(grid4, BF16), vm(small4, F32),
+        vm(grid4, BF16), vm(grid4, BF16), vm(grid4, BF16), vm((n_head, 16, 2 * LANES), BF16),
         vm((pieces, state, GROUP), BF16), vm((pieces, state, GROUP), BF16),
         vm(grid4, BF16),
         dma((n_head,)), dma((n_head,)), dma((n_head,)), dma((n_head,)),
         dma, dma,
-        dma((n_head, pieces)), dma((n_head, pieces)), dma((n_head, pieces)), dma((n_head, pieces)),
+        dma((n_head, pieces)), dma((n_head, pieces)), dma((n_head,)), dma((n_head,)),
         dma((pieces,)), dma((pieces,)),
         dma((n_head, pieces)), dma((n_head, pieces)),
         dma((n_head,)), dma, dma((n_head * pieces,)), dma, dma((pieces,)),

time: 66.4 us -> 61.2 us (0.922); the launches traced: 66.2 us -> 60.1 us
  Pallas kernels: 66.2 us -> 60.1 us
    pallas_call x1, Pallas kernels: 58.4 us -> 52.4 us  [per_device(): pl.pallas_call(functools.partial(kernel, n_ctx, n_head, heads, width, pie...]
where the time goes in v5:
time: 61.2 us; the launch traced here: 60.1 us
  Pallas kernels  60.1 us (98%)
    pallas_call x1, Pallas kernels, per_device(): pl.pallas_call(functools.partial(kernel, n_ctx, n_head, heads, width, pie...  52.4 us
    pallas_call x1, Pallas kernels, per_device(): pl.pallas_call(functools.partial(finish, width), grid=(n_head,), out_shap...  7.77 us

profile of v5, /device:TPU:28, one launch (start us, length us, event | category | flops | bytes accessed | tf_op | source)
XLA Modules:
  0.0 60.1 jit_solution(157273319288324507)
XLA Ops:
  0.0 52.4 %ssd_layer.1 = (bf16[512,5120]{1,0:T(8,128)(2,1)}, bf16[4,5,128,256]{3,2,1,0:T(8,128)(2,1)}, bf16[4,5,128,256]{3,2,1,0:T(8,128)(2,1)}, f32[4,5,8,256]{3,2,1,0:T(...) custom-call(bf16[512,5120]{1,0:T(8,128)(2,1)} %x_hbm.1, bf16[512,256]{1,0:T(8,128)(2,1)} %si_ref.1, ...), custom_call_target="tpu_custom_call" | custom-call | tf_op jit(solution)/shard_map/ssd_layer/pallas_call | solution.py:455
  52.4 7.8 %carried_terms.1 = bf16[512,5120]{1,0:T(8,128)(2,1)} custom-call(bf16[512,5120]{1,0:T(8,128)(2,1)} %get-tuple-element.11.acc_ref, bf16[4,5,128,256]{3,2,1,0:T(8,128)(2,1)} %get-tuple-element.12.inc_ref, bf16[4,5,128,256]{3,2,1,0:T(8,128)(2,1)} %get-tuple-element.13.s0_ref, f32[4,5,8,256]{3,2,1,0:T(8,128)} %get-tuple-element.14.dx_ref, ...), custom_call_target="tpu_custom_call" | custom-call | tf_op jit(solution)/shard_map/carried_terms/pallas_call | solution.py:471
